TPU v7x, 128 devices: a whole 4x4x4 slice. The times are simulated.
128 devices in a mesh: row: 16 (over x, z), col: 8 (over y, core).
Axes of the slice: x: 4, y: 4, z: 4, core: 2. Of those that a mesh axis runs over, the one named last changes fastest.
Arguments:
- root_inverse: float32 [2, 2048, 4, 1024], P(None, 'row', None, 'col'), as said below
- child_coupling: float32 [2, 2, 2048, 2, 1024], P(None, None, 'row', None, 'col'), may hold values from -0.046875 to 0.046875
- child_inverse: float32 [2, 1, 2048, 2, 1024], P(None, None, 'row', None, 'col'), as said below
- pattern: int32 [2, 32], replicated, may hold values 0 or 1
Outputs:
- sigma_root: float32 [2, 2048, 4, 1024], P(None, 'row', None, 'col')
- sigma_coupling: float32 [2, 2, 2048, 2, 1024], P(None, None, 'row', None, 'col')
- sigma_child: float32 [2, 128, 2, 1024], P(None, None, None, 'col')
Inputs may be any that keep to these rules, and one draw needn't show every extreme that they name: `root_inverse`: read row-major as a 4096 x 4096 matrix it is lower triangular with a positive diagonal. `child_inverse`: read row-major each child's 2048 x 2048 matrix is lower triangular with a positive diagonal. `pattern`: 1 where child j's separator couples to root supernode i, else 0.
All inputs are finite; a program needn't handle non-finite values.
Results may differ from a plain program's by a relative error of at most 0.00013.
Values sent between devices are 32-bit elements; how exact they have to be, the bound alone decides.
No kernel may reach another device: no remote copies, remote signals or barrier semaphores. Data moves between devices by JAX's collectives and lax.ppermute only.
A program may use at most 128 MiB of HBM per device.

v0:
```python
import jax
import jax.numpy as jnp
from jax import lax
from jax.sharding import PartitionSpec as P

B = 128
NR = 4096
NC = 2048


def spread(value, axis, source):
    kept = jnp.where(lax.axis_index(axis) == source, value, 0).astype(value.dtype)
    return lax.psum(kept, axis)


def local(root_inverse, child_coupling, child_inverse, pattern):
    highest = lax.Precision.HIGHEST
    rows_axis = lax.axis_size("row")
    cols_axis = lax.axis_size("col")
    my_row = lax.axis_index("row")
    root_blocks, width, col_blocks, _ = root_inverse.shape
    child_count = child_coupling.shape[0]
    child_columns = child_coupling.shape[3]
    local_rows = root_blocks * width
    block_ids = jnp.arange(root_blocks, dtype=jnp.int32) * rows_axis + my_row
    matches = (jnp.arange(NR // B, dtype=jnp.int32)[None, :] == block_ids[:, None]).astype(
        jnp.float32
    )
    keep = jnp.einsum("jn,an->ja", pattern.astype(jnp.float32), matches)
    coupled = child_coupling * keep[:, :, None, None, None]
    root_panel, child_panel = (
        lax.all_gather(root_inverse, "row", axis=1, tiled=True),
        lax.all_gather(child_inverse, "row", axis=2, tiled=True),
    )
    columns = root_panel.reshape(NR, col_blocks * width)
    groups = rows_axis // cols_axis
    chosen = lax.dynamic_index_in_dim(
        columns.reshape(NR, root_blocks, groups, width), my_row // cols_axis, 2, False
    )
    mirrored = spread(chosen.reshape(NR, local_rows), "col", my_row % cols_axis)
    sigma_local = jnp.einsum("km,kn->mn", mirrored, columns, precision=highest)
    sigma_root = sigma_local.reshape(root_blocks, width, col_blocks, width)
    sigma_rows, coupling_rows = (
        lax.all_gather(sigma_root, "col", axis=3, tiled=True),
        lax.all_gather(coupled, "col", axis=4, tiled=True),
    )
    coupling_panel = coupling_rows.reshape(child_count, local_rows, NC)
    inverse_columns = child_panel.reshape(child_count, NC, child_columns * width)
    update = jnp.einsum("jmk,jkn->jmn", coupling_panel, inverse_columns, precision=highest)
    sigma_split = sigma_rows.reshape(local_rows, root_blocks, rows_axis * width)
    update_split = update.reshape(child_count, root_blocks, width, child_columns * width)
    product = jnp.einsum(
        "mak,jakn->jmn",
        sigma_split,
        lax.all_gather(update_split, "row", axis=2, tiled=True),
        precision=highest,
    )
    coupling_sigma = -(
        product.reshape(child_count, root_blocks, width, child_columns * width)
        * keep[:, :, None, None]
    )
    local_inverse = child_inverse.reshape(child_count, -1, child_columns, width)
    first_part = jnp.einsum("jkcr,jkcs->jcrs", local_inverse, local_inverse, precision=highest)
    update_blocks = update.reshape(child_count, local_rows, child_columns, width)
    sigma_blocks = coupling_sigma.reshape(child_count, local_rows, child_columns, width)
    second_part = jnp.einsum("jkcr,jkcs->jcrs", update_blocks, sigma_blocks, precision=highest)
    summed = lax.psum(first_part - second_part, "row")
    sigma_child = summed.transpose(0, 2, 1, 3)
    return (
        sigma_root,
        coupling_sigma.reshape(child_count, root_blocks, width, child_columns, width),
        sigma_child,
    )


def solution(mesh):
    in_specs = (
        P(None, "row", None, "col"),
        P(None, None, "row", None, "col"),
        P(None, None, "row", None, "col"),
        P(),
    )
    out_specs = (
        P(None, "row", None, "col"),
        P(None, None, "row", None, "col"),
        P(None, None, None, "col"),
    )
    return jax.shard_map(local, mesh=mesh, in_specs=in_specs, out_specs=out_specs, check_vma=False)
```

profile of v0, /device:TPU:0, one launch (start us, length us, event | category | flops | bytes accessed | tf_op | source)
XLA Modules:
  0.0 490.8 jit_solution(11845554919135694700)
XLA Ops:
  7.2 0.7 all-gather.6.cloned.1.call-update
  8.0 75.6 %all-gather.6.cloned.1.call-done = f32[2,2048,4,128]{3,2,1,0:T(4,128)} async-done(((f32[2,128,4,128]{3,2,1,0:T(4,128)}), f32[2,2048,4,128]{3,2,1,0:T(4,128)}) %all-gather.6.cloned.1.call-update) | async-done | bytes 8388624 | tf_op jit(solution)/shard_map/all_gather | solution.py:32
  83.6 7.3 %broadcast_select_fusion = f32[4096,2,1,128]{3,2,1,0:T(1,128)} fusion(pred[]{:T(512)S(6)} %eq.18, f32[4096,2,2,128]{3,2,1,0:T(2,128)} %bitcast.53, s32[]{:T(128)S(6)} %select_n.29), kind=kLoop, calls=%fused_computation.1 | loop fusion | flops 1048576 | bytes 8388613 | tf_op jit(solution)/shard_map/jit(_where)/select_n | solution.py:12
  90.8 10.2 %copy.19 = f32[4096,2,1,128]{0,3,1,2:T(8,128)} copy(f32[4096,2,1,128]{3,2,1,0:T(1,128)} %broadcast_select_fusion) | data formatting | bytes 8388608 | tf_op jit(solution)/shard_map/jit(_where)/select_n | solution.py:12
  101.1 0.6 copy-done.3
  102.1 1.0 broadcast_multiply_fusion
  103.2 0.5 all-gather.10.cloned.1.call-update
  103.7 7.6 %copy.44 = f32[512,8,4,128]{3,1,2,0:T(8,128)} copy(f32[512,8,4,128]{3,2,1,0:T(4,128)} %bitcast.54) | data formatting | bytes 16777216
  111.3 9.0 %copy.20 = f32[4096,512]{0,1:T(8,128)} copy(f32[4096,512]{1,0:T(8,128)} %bitcast.52) | data formatting | bytes 16777216 | tf_op jit(solution)/shard_map/reshape | solution.py:35
  120.3 53.0 %all-reduce.3.cloned.1.call-done = f32[2,128,4096]{2,1,0:T(8,128)} async-done(((f32[2,128,4096]{2,1,0:T(8,128)}), f32[2,128,4096]{2,1,0:T(8,128)}) %all-reduce.3.cloned.1.call-update) | async-done | bytes 4194320 | tf_op jit(solution)/shard_map/psum | solution.py:13
  173.3 11.0 %fusion = f32[2,128,4,128]{3,1,2,0:T(8,128)} fusion(f32[4,128,4096,1]{2,1,0,3:T(8,128)} %bitcast.51, f32[2,128,4096]{2,1,0:T(8,128)} %all-reduce.3.cloned.1.call-done), kind=kOutput, calls=%fused_computation.2 | convolution fusion | flops 6442450944 | bytes 13107200 | tf_op jit(solution)/shard_map/km,kn->mn/dot_general | solution.py:41
  184.4 27.3 %all-gather.8.cloned.1.call-done = f32[2,2,128,2,1024]{4,3,2,1,0:T(2,128)} async-done(((f32[2,2,128,2,128]{4,3,2,1,0:T(2,128)}), f32[2,2,128,2,1024]{4,3,2,1,0:T(2,128)}) %all-gather.8.cloned.1.call-update) | async-done | bytes 4194320 | tf_op jit(solution)/shard_map/all_gather | solution.py:45
  211.7 6.6 %reshape.53 = f32[2,256,2048]{2,1,0:T(8,128)} reshape(f32[2,2,128,2,1024]{4,3,2,1,0:T(2,128)} %all-gather.8.cloned.1.call-done) | data formatting | bytes 8388608 | tf_op jit(solution)/shard_map/reshape | solution.py:47
  218.3 48.1 %all-gather.10.cloned.1.call-done = f32[2,1,2048,2,128]{4,3,2,1,0:T(2,128)} async-done(((f32[2,1,128,2,128]{4,3,2,1,0:T(2,128)}), f32[2,1,2048,2,128]{4,3,2,1,0:T(2,128)}) %all-gather.10.cloned.1.call-update) | async-done | bytes 4194320 | tf_op jit(solution)/shard_map/all_gather | solution.py:33
  266.4 6.4 %reshape.54 = f32[2,2048,256]{2,1,0:T(8,128)} reshape(f32[2,1,2048,2,128]{4,3,2,1,0:T(2,128)} %all-gather.10.cloned.1.call-done) | data formatting | bytes 8388608 | tf_op jit(solution)/shard_map/reshape | solution.py:48
  272.9 8.1 %fusion.14 = f32[2,256,256]{2,1,0:T(8,128)S(1)} fusion(f32[2,256,2048]{2,1,0:T(8,128)} %reshape.53, f32[2,2048,256]{2,1,0:T(8,128)} %reshape.54), kind=kOutput, calls=%fused_computation.23 | convolution fusion | flops 3221225472 | bytes 8912896 | tf_op jit(solution)/shard_map/jmk,jkn->jmn/dot_general | solution.py:49
  280.9 1.0 copy.22
  282.0 0.2 all-reduce.5.cloned.1.call-start
  282.3 0.2 copy.37
  282.5 21.7 %all-gather.14.cloned.1.call-done = f32[2,128,4,1024]{3,1,2,0:T(8,128)} async-done(((f32[2,128,4,128]{3,1,2,0:T(8,128)}), f32[2,128,4,1024]{3,1,2,0:T(8,128)}) %all-gather.14.cloned.1.call-update) | async-done | bytes 4194320 | tf_op jit(solution)/shard_map/all_gather | solution.py:44
  304.2 7.3 %copy.23 = f32[2,128,4,1024]{1,0,3,2:T(2,128)} copy(f32[2,128,4,1024]{3,1,2,0:T(8,128)} %all-gather.14.cloned.1.call-done) | data formatting | bytes 8388608 | tf_op jit(solution)/shard_map/all_gather | solution.py:44
  311.5 6.4 %reshape.56 = f32[256,2,2048]{0,2,1:T(8,128)} reshape(f32[2,128,4,1024]{1,0,3,2:T(2,128)} %copy.23) | data formatting | bytes 8388608 | tf_op jit(solution)/shard_map/reshape | solution.py:50
  317.9 68.3 %all-gather.12.cloned.1.call-done = f32[2,2,2048,256]{2,3,1,0:T(8,128)} async-done(((f32[2,2,128,256]{2,3,1,0:T(8,128)}), f32[2,2,2048,256]{2,3,1,0:T(8,128)}) %all-gather.12.cloned.1.call-update) | async-done | bytes 8388624 | tf_op jit(solution)/shard_map/all_gather | solution.py:55
  386.2 9.8 %fusion.2 = f32[2,256,256,1]{2,1,3,0:T(8,128)S(1)} fusion(f32[2,2,2048,256]{2,3,1,0:T(8,128)} %all-gather.12.cloned.1.call-done, f32[256,2,2048]{0,2,1:T(8,128)} %reshape.56), kind=kOutput, calls=%fused_computation.4 | convolution fusion | flops 6442450944 | bytes 13107200 | tf_op jit(solution)/shard_map/mak,jakn->jmn/dot_general | solution.py:52
  396.2 0.8 fusion.5
  397.0 1.3 fusion.4
  398.3 1.1 copy.31
  399.5 0.3 reshape.57
  399.7 0.4 copy.25
  400.2 1.1 multiply_negate_fusion
  401.2 80.9 %all-reduce.5.cloned.1.call-done = f32[2,128,2,128]{3,1,2,0:T(8,128)} async-done(((f32[2,128,2,128]{3,1,2,0:T(8,128)}), f32[2,128,2,128]{3,1,2,0:T(8,128)}) %all-reduce.5.cloned.1.call-update) | async-done | bytes 262160 | tf_op jit(solution)/shard_map/psum | solution.py:67
  482.1 1.9 copy.32
  (24 shorter events, 1.0 us)
Async XLA Ops:
  7.2 76.4 %all-gather.6.cloned.1.call-start = ((), (), s32[]{:S(2)}) async-start(), calls=%async_computation | async-start | bytes 8912896 | tf_op jit(solution)/shard_map/all_gather | solution.py:32
  7.9 165.4 %all-reduce.3.cloned.1.call-start = ((), (), s32[]{:S(2)}) async-start(), calls=%async_computation.1 | async-start | bytes 8388608 | tf_op jit(solution)/shard_map/psum | solution.py:13
  101.0 0.7 copy-start.3
  101.0 1.1 copy-start.2
  101.0 110.6 %all-gather.8.cloned.1.call-start = ((), (), s32[]{:S(2)}) async-start(), calls=%async_computation.2 | async-start | bytes 4718592 | tf_op jit(solution)/shard_map/all_gather | solution.py:45
  103.1 163.3 %all-gather.10.cloned.1.call-start = ((), (), s32[]{:S(2)}) async-start(), calls=%async_computation.3 | async-start | bytes 4456448 | tf_op jit(solution)/shard_map/all_gather | solution.py:33
  103.7 200.5 %all-gather.14.cloned.1.call-start = ((), (), s32[]{:S(2)}) async-start(), calls=%async_computation.5 | async-start | bytes 4718592 | tf_op jit(solution)/shard_map/all_gather | solution.py:44
  184.3 201.9 %all-gather.12.cloned.1.call-start = ((), (), s32[]{:S(2)}) async-start(), calls=%async_computation.4 | async-start | bytes 8912896 | tf_op jit(solution)/shard_map/all_gather | solution.py:55
  282.0 200.1 %all-reduce.5.cloned.1.call-start = ((), (), s32[]{:S(2)}) async-start(), calls=%async_computation.6 | async-start | bytes 524288 | tf_op jit(solution)/shard_map/psum | solution.py:67
  317.9 79.1 %copy-start.1 = (f32[2,1,128,2,128]{4,3,2,1,0:T(2,128)S(1)}, f32[2,1,128,2,128]{4,3,2,1,0:T(2,128)}, u32[]{:S(2)}) copy-start(f32[2,1,128,2,128]{4,3,2,1,0:T(2,128)} %param.6) | copy-start | bytes 786436
  317.9 80.4 %copy-start = (f32[2,128,4,128]{3,1,2,0:T(8,128)S(1)}, f32[2,128,4,128]{3,1,2,0:T(8,128)}, u32[]{:S(2)}) copy-start(f32[2,128,4,128]{3,1,2,0:T(8,128)} %fusion) | copy-start | bytes 1572868
Sparse Core Ops, SparseCore 0:
  10.2 73.3 all-gather.5
  101.1 72.0 all-reduce.2
  175.5 36.0 all-gather.7
  213.7 52.6 all-gather.9
  268.5 35.6 all-gather.13
  306.7 79.4 all-gather.11
  398.4 83.6 all-reduce.4
where the time goes:
time: 492 us; the launch traced here: 491 us
  waiting for transfers between devices  376 us (76%)
  local copies, waits for them, and re-layouts  59.4 us (12%)
  matrix products  31.1 us (6%)
  between operations  14.2 us (3%)
  other arithmetic  9.37 us (2%)
    psum x1, waiting for transfers between devices, local(): summed = lax.psum(first_part - second_part, 'row')  80.9 us
    all_gather x1, waiting for transfers between devices, local(): lax.all_gather(root_inverse, 'row', axis=1, tiled=True)  75.6 us
    all_gather x1, waiting for transfers between devices, local(): lax.all_gather(update_split, 'row', axis=2, tiled=True)  68.3 us
    psum x1, waiting for transfers between devices, spread(): return lax.psum(kept, axis)  53 us
    all_gather x1, waiting for transfers between devices, local(): lax.all_gather(child_inverse, 'row', axis=2, tiled=True)  48.1 us
    all_gather x1, waiting for transfers between devices, local(): lax.all_gather(coupled, 'col', axis=4, tiled=True)  27.3 us
    all_gather x1, waiting for transfers between devices, local(): lax.all_gather(sigma_root, 'col', axis=3, tiled=True)  21.7 us
    unnamed x13, local copies, waits for them, and re-layouts  11.4 us
  transfers between devices with their start and end apart: 7, of which 7 were waited for; matrix products, arithmetic and copies ran while one was open for 14% of the time, Pallas kernels for 0%

commit v1 on v0

v1 whole, which is shorter than its diff:
```python
import functools

import jax
import jax.numpy as jnp
from jax import lax
from jax.experimental import pallas as pl
from jax.experimental.pallas import tpu as pltpu
from jax.sharding import PartitionSpec as P

X, Z, Y, CORES = 4, 4, 4, 2
W = 128
F32, BF16 = jnp.float32, jnp.bfloat16
AXES = ("row", "col")


def moves(target):
    pairs = []
    for x in range(X):
        for z in range(Z):
            for y in range(Y):
                for core in range(CORES):
                    there = target(x, z, y, core)
                    if there is not None:
                        u, w, v, k = there
                        pairs.append((((x * Z + z) * Y + y) * CORES + core, ((u * Z + w) * Y + v) * CORES + k))
    return pairs


ALONG_X = [moves(lambda x, z, y, k, n=n: ((x + n * (1 - 2 * k)) % X, z, y, k)) for n in (1, -1)]
ALONG_Z = [moves(lambda x, z, y, k, n=n: (x, (z + n * (1 - 2 * k)) % Z, y, k)) for n in (1, -1)]
FLIP_X = [moves(lambda x, z, y, k, n=n: (x ^ (n if k == 0 else 4 - n), z, y, k)) for n in (1, 3)]
FLIP_Z = [moves(lambda x, z, y, k, n=n: (x, z ^ (n if k == 0 else 4 - n), y, k)) for n in (1, 3)]
FOLD = moves(lambda x, z, y, k: (3 - x, z, y, k) if x >= 2 else None)


def mirror(first):
    def target(x, z, y, k):
        r, c = x * Z + z, y * CORES + k
        to = c if (r % 2 == 0) == first else c + 8
        return to // Z, to % Z, (r // 2) // CORES, (r // 2) % CORES

    return moves(target)


MIRROR_1, MIRROR_2 = mirror(True), mirror(False)


def send(value, pairs):
    return lax.ppermute(value, AXES, pairs)


def after(value, *others):
    return lax.optimization_barrier((value, *others))[0]


def ring(value, pairs, *others):
    near = send(value, pairs[0])
    return [value, near, send(value, pairs[1]), send(after(near, *others) if others else near, pairs[0])]


def stack_kernel(*refs):
    sources, outs, semaphores = refs[:8], refs[8:10], refs[10]
    rows = sources[0].shape[0]
    copies = [
        pltpu.make_async_copy(source, outs[n // 4].at[pl.ds((n % 4) * rows, rows)], semaphores.at[n]) for n, source in enumerate(sources)
    ]
    for copy in copies:
        copy.start()
    for copy in copies:
        copy.wait()


def gather(value_x, value_z, *others):
    rings = ring(value_x, ALONG_X, *others) + ring(value_z, ALONG_Z, *others)
    four_x, four_z = pl.pallas_call(
        stack_kernel,
        out_shape=(shape(4 * value_x.shape[0], value_x.shape[1]),) * 2,
        in_specs=[pl.BlockSpec(memory_space=pl.ANY)] * 8,
        out_specs=(pl.BlockSpec(memory_space=pltpu.VMEM),) * 2,
        scratch_shapes=[pltpu.SemaphoreType.DMA((8,))],
        compiler_params=pltpu.CompilerParams(vmem_limit_bytes=8 << 20),
    )(*rings)
    return ring(four_x, ALONG_Z), ring(four_z, ALONG_X), four_x


def place():
    row, core = lax.axis_index("row"), lax.axis_index("col") % 2
    return row // 4, row % 4, 1 - 2 * core


def origin(index, step, d):
    return (index + 4 + (0, -d, d, 2)[step]) % 4


def step_of(there, here, d):
    offset = ((there - here) * d + 8) % 4
    return jnp.where(offset == 3, 1, jnp.where(offset == 0, 0, offset + 1))


def at(index, size):
    return pl.ds(pl.multiple_of(index * size, size), size)


def split(value):
    high = value.astype(BF16)
    return high, (value - high.astype(F32)).astype(BF16)


def put(high, low, where, value):
    h, l = split(value)
    high[where] = h
    low[where] = l


def dot3(left, right):
    dot = functools.partial(jnp.dot, preferred_element_type=F32)
    return dot(left[0], right[0]) + (dot(left[0], right[1]) + dot(left[1], right[0]))


class Staged:
    def __init__(self, source, buffer, semaphore):
        self.copy, self.buffer, self.shape, self.here = pltpu.make_async_copy(source, buffer, semaphore), buffer, buffer.shape, False
        self.copy.start()

    def __getitem__(self, where):
        if not self.here:
            self.copy.wait()
            self.here = True
        return self.buffer[where]


def call(kernel, outs, operands, scratch=(), scalars=(), flops=0, vmem=56):
    operands = [v if isinstance(v, tuple) else (v, None) for v in operands]
    ranges, operands = [v[1] for v in operands], [v[0] for v in operands]
    shapes = [v.shape if cols is None else (v.shape[0], cols[1] - cols[0]) for v, cols in zip(operands, ranges)]
    n, m = len(scalars), len(operands)

    def body(*refs):
        first, sources, rest = refs[:n], refs[n : n + m], refs[n + m :]
        results, rest = rest[: len(outs)], rest[len(outs) :]
        buffers, semaphores, rest = rest[:m], rest[m], rest[m + 1 :]
        sources = [v if cols is None else v.at[:, pl.ds(cols[0], cols[1] - cols[0])] for v, cols in zip(sources, ranges)]
        staged = [Staged(source, buffer, semaphores.at[t]) for t, (source, buffer) in enumerate(zip(sources, buffers))]
        kernel(*first, *staged, *results, *rest)

    return pl.pallas_call(
        body,
        out_shape=outs,
        in_specs=[pl.BlockSpec(memory_space=pltpu.SMEM)] * n + [pl.BlockSpec(memory_space=pl.ANY)] * m,
        out_specs=tuple(pl.BlockSpec(memory_space=pltpu.VMEM) for _ in outs),
        scratch_shapes=[pltpu.VMEM(dims, v.dtype) for v, dims in zip(operands, shapes)] + [pltpu.SemaphoreType.DMA((m,))] + list(scratch),
        compiler_params=pltpu.CompilerParams(vmem_limit_bytes=vmem << 20),
        cost_estimate=pl.CostEstimate(flops=flops, bytes_accessed=1 << 22, transcendentals=0),
    )(*scalars, *operands)


def shape(*dims, dtype=F32):
    return jax.ShapeDtypeStruct(dims, dtype)


def cut_kernel(pattern, a, c, k, by_x, own_z, fold, cw, m1, m2):
    row = lax.axis_index("row")

    def block_a(i, q):
        return a[pl.ds(i * 512 + q, W, stride=4), :]

    def block_k(j, q):
        return k[pl.ds(j * 256 + q, W, stride=2), :]

    def lay(out, *blocks):
        for n, block in enumerate(blocks):
            out[:, n * W : (n + 1) * W] = block

    lay(by_x, block_k(0, 0), block_k(1, 0), block_a(1, 0), block_a(1, 1))
    lay(own_z, block_a(1, 3), block_k(1, 1), block_a(1, 2), block_a(0, 0))
    lay(fold, block_a(0, 1), block_k(0, 1))
    for j in range(2):
        for i in range(2):
            kept = pattern[j, row + 16 * i].astype(F32)
            for q in range(2):
                block = c[pl.ds((j * 2 + i) * 256 + q, W, stride=2), :]
                cw[pl.ds((j * 2 + i) * W, W), q * W : (q + 1) * W] = block * kept
    even = row % 2 == 0
    for m, (i, q) in enumerate(((0, 0), (1, 0), (1, 2))):
        low, high = block_a(i, q).T, block_a(i, q + 1).T
        m1[pl.ds(m * W, W), :] = jnp.where(even, low, high)
        m2[pl.ds(m * W, W), :] = jnp.where(even, high, low)


def block_of(pieces, b, cols):
    return pieces[b // 4][pl.ds((b % 4) * W, W), cols]


def fold_home(from_x, from_z):
    kind = (from_x >= 2).astype(jnp.int32)
    return kind, jnp.where(from_x < 2, 1 - from_x, from_x - 2) * 4 + from_z


def rows_kernel(cw, high, low):
    for column in range(8):
        for q in range(2):
            for j in range(2):
                here = (j, slice(None), slice((column + 8 * q) * W, (column + 8 * q + 1) * W))
                put(high, low, here, cw[column, pl.ds(j * 256, 256), q * W : (q + 1) * W])


def update_kernel(high, low, *refs):
    by_x, by_z = refs[:4], refs[4:8]
    (u0, u1), (rh, rl, eh, el) = refs[8:10], refs[10:]
    x, z, d = place()
    for b in range(16):
        row = origin(x, b % 4, d) * 4 + origin(z, b // 4, d)
        put(rh, rl, (at(row, W), slice(None)), block_of(by_x, b, slice(None)))
        kind, row = fold_home(origin(x, b // 4, d), origin(z, b % 4, d))
        put(eh, el, (kind, at(row, W), slice(None)), block_of(by_z, b, slice(None)))
    everything, upper = slice(None), slice(1024, 2048)
    for j in range(2):
        cols = slice(j * W, (j + 1) * W)
        first = dot3((high[j, :, everything], low[j, :, everything]), (rh[:, cols], rl[:, cols]))
        second = dot3((high[j, :, upper], low[j, :, upper]), (eh[j], el[j]))
        for i, u in enumerate((u0, u1)):
            u[:, 2 * j * W : (2 * j + 1) * W] = first[i * W : (i + 1) * W]
            u[:, (2 * j + 1) * W : (2 * j + 2) * W] = second[i * W : (i + 1) * W]


def root_kernel(m, *refs):
    by_x, by_z = refs[:4], refs[4:8]
    (s_out, root_out), (h0, l0, h1, l1, rh, rl, r0h, r0l, eh, el) = refs[8:10], refs[10:]
    x, z, d = place()
    upper = (4 * x + z >= 8).astype(jnp.int32)
    for column in range(8):
        for n in range(2):
            here = at(2 * column + (n + upper) % 2, W)
            for part, (hr, lr, lo) in enumerate(((h0, l0, 0), (h1, l1, 0), (h1, l1, W))):
                put(hr, lr, (pl.ds(lo, W), here), m[column, pl.ds((n * 3 + part) * W, W), :])
    for b in range(16):
        row = origin(x, b % 4, d) * 4 + origin(z, b // 4, d)
        put(rh, rl, (at(row, W), slice(0, 2 * W)), block_of(by_x, b, slice(None)))
        from_x, from_z = origin(x, b // 4, d), origin(z, b % 4, d)
        row = 4 * from_x + from_z
        put(rh, rl, (at(row, W), slice(2 * W, 3 * W)), block_of(by_z, b, slice(2 * W, 3 * W)))
        put(r0h, r0l, (at(row, W), slice(None)), block_of(by_z, b, slice(3 * W, 4 * W)))
        kind, row = fold_home(from_x, from_z)
        put(eh, el, (kind, at(row, W), slice(None)), block_of(by_z, b, slice(0, W)))
    late = slice(1024, 2048)
    s_out[:, : 3 * W] = dot3((h1[...], l1[...]), (rh[...], rl[...]))
    s_out[:, 3 * W :] = dot3((h1[:, late], l1[:, late]), (eh[1], el[1]))
    s_out[:W, :W] += dot3((h0[...], l0[...]), (r0h[...], r0l[...]))
    s_out[:W, W : 2 * W] += dot3((h0[:, late], l0[:, late]), (eh[0], el[0]))
    for i in range(2):
        for q in range(4):
            root_out[pl.ds(i * 512 + q, W, stride=4), :] = s_out[pl.ds(i * W, W), q * W : (q + 1) * W]


def halves_kernel(*refs):
    for n in range(6):
        put(refs[6], refs[7], (pl.ds(n * 512, 512), slice(None)), refs[n][...])


def product_kernel(pattern, s_in, early_high, early_low, *refs):
    late, (u0, u1, k), (p_out, *g_out), (high, low) = refs[:2], refs[2:5], refs[5:8], refs[8:]
    row = lax.axis_index("row")
    x, z, d = place()
    for column in range(8):
        for q in range(4):
            block = column + 8 * (q % 2)
            along_x, along_z = step_of(block // 4, x, d), step_of(block % 4, z, d)
            block = along_x + 4 * along_z if q < 2 else 16 + along_z + 4 * along_x
            put(high, low, (slice(None), at(block, W)), s_in[column, :, q * W : (q + 1) * W])
    total = jnp.zeros((256, 512), F32)
    for n in range(2):
        part, rows = slice(n * 2048, n * 2048 + 1536), slice(n * 1536, (n + 1) * 1536)
        total = total + dot3((high[:, part], low[:, part]), (early_high[rows, :], early_low[rows, :]))
        part = slice(n * 2048 + 1536, (n + 1) * 2048)
        total = total + dot3((high[:, part], low[:, part]), split(late[n][...]))
    for j in range(2):
        for q in range(2):
            cols = slice((2 * j + q) * W, (2 * j + q + 1) * W)
            own = k[pl.ds(j * 256 + q, W, stride=2), :]
            block = dot3(split(own.T), split(own))
            for i, u in enumerate((u0, u1)):
                scaled = total[i * W : (i + 1) * W, cols] * -pattern[j, row + 16 * i].astype(F32)
                p_out[pl.ds((j * 2 + i) * 256 + q, W, stride=2), :] = scaled
                block = block - dot3(split(u[:, cols].T), split(scaled))
            g_out[j][pl.ds(q, W, stride=2), :] = block


def local(root_inverse, child_coupling, child_inverse, pattern):
    a = root_inverse.reshape(1024, W)
    c = child_coupling.reshape(1024, W)
    k = child_inverse.reshape(512, W)
    by_x, own_z, fold, cw, m1, m2 = call(
        cut_kernel,
        (shape(W, 512), shape(W, 512), shape(W, 256), shape(512, 256), shape(384, W), shape(384, W)),
        (a, c, k),
        scalars=(pattern,),
    )

    folded = jnp.where(lax.axis_index("row") >= 8, own_z[:, : 2 * W], send(fold, FOLD))
    by_z = jnp.concatenate([folded, own_z[:, 2 * W :]], axis=1)
    m1, m2 = send(m1, MIRROR_1), send(m2, MIRROR_2)
    x_parts, z_parts, four = gather(by_x, by_z, m1, m2)
    mirrored = lax.all_gather(jnp.concatenate([after(m1, four), after(m2, four)], axis=0), "col")
    coupling = lax.all_gather(cw, "col")
    rows = call(rows_kernel, (shape(2, 256, 2048, dtype=BF16),) * 2, (coupling,), flops=1 << 20)
    u0, u1 = call(
        update_kernel,
        (shape(W, 512),) * 2,
        (*rows, *((v, (0, 256)) for v in x_parts), *((v, (128, 256)) for v in z_parts)),
        scratch=[pltpu.VMEM((2048, 256), BF16)] * 2 + [pltpu.VMEM((2, 1024, W), BF16)] * 2,
        flops=1 << 31,
    )

    first, second, begun = gather(u0, u1)
    sigma, sigma_root = call(
        root_kernel,
        (shape(256, 512), shape(1024, W)),
        (after(mirrored, begun), *((v, (256, 512)) for v in x_parts), *z_parts),
        scratch=[pltpu.VMEM((W, 2048), BF16)] * 2
        + [pltpu.VMEM((256, 2048), BF16)] * 2
        + [pltpu.VMEM((2048, 384), BF16)] * 2
        + [pltpu.VMEM((2048, W), BF16)] * 2
        + [pltpu.VMEM((2, 1024, W), BF16)] * 2,
        flops=1 << 31,
    )
    early = call(halves_kernel, (shape(3072, 512, dtype=BF16),) * 2, (*first[:3], *second[:3]), flops=1 << 36)
    p, g0, g1 = call(
        product_kernel,
        (shape(1024, W), shape(256, W), shape(256, W)),
        (lax.all_gather(sigma, "col"), *early, first[3], second[3], u0, u1, k),
        scalars=(pattern,),
        scratch=[pltpu.VMEM((256, 4096), BF16)] * 2,
        flops=1 << 30,
    )
    for along_x, along_z in zip(FLIP_X + FLIP_Z, FLIP_Z + FLIP_X):
        g0, g1 = g0 + send(g0, along_x), g1 + send(g1, along_z)
    g = jnp.concatenate([g0, g1], axis=0)
    return sigma_root.reshape(2, W, 4, W), p.reshape(2, 2, W, 2, W), g.reshape(2, W, 2, W)


def solution(mesh):
    in_specs = (
        P(None, "row", None, "col"),
        P(None, None, "row", None, "col"),
        P(None, None, "row", None, "col"),
        P(),
    )
    out_specs = (
        P(None, "row", None, "col"),
        P(None, None, "row", None, "col"),
        P(None, None, None, "col"),
    )
    return jax.shard_map(local, mesh=mesh, in_specs=in_specs, out_specs=out_specs, check_vma=False)
```

time: 492 us -> 217 us (0.44)
  waiting for transfers between devices: 376 us -> 90.4 us
  starting transfers between devices: 0.46 us -> 65.1 us
  local copies, waits for them, and re-layouts: 59.4 us -> 2.87 us
  Pallas kernels: 0 us -> 39.2 us
  matrix products: 31.1 us -> 0 us
    all_gather x5 -> x3, waiting for transfers between devices: 241 us -> 4.46 us  [the longest x1 4.46 us: local(): lax.all_gather(sigma, 'col')]
    psum x2 -> x0, waiting for transfers between devices: 134 us -> none  [the longest x1 80.9 us: local(): summed = lax.psum(first_part - second_part, 'row')]
    ppermute x0 -> x35, waiting for transfers between devices: none -> 85.9 us  [send(): return lax.ppermute(value, AXES, pairs)]
    ppermute x0 -> x35, starting transfers between devices: none -> 65 us  [send(): return lax.ppermute(value, AXES, pairs)]
    pallas_call x0 -> x8, Pallas kernels: none -> 39.2 us  [the longest x6 38.7 us: call(): pl.pallas_call(body, out_shape=outs, in_specs=[pl.BlockSpec(memory_space=...]
    dot_general x6 -> x0, matrix products: 31.1 us -> none  [the longest x1 11 us: local(): sigma_local = jnp.einsum('km,kn->mn', mirrored, columns, precision=highest)]
    reshape x9 -> x0, local copies, waits for them, and re-layouts: 30.5 us -> none  [the longest x1 8.97 us: local(): columns = root_panel.reshape(NR, col_blocks * width)]
    select_n x1 -> x0, local copies, waits for them, and re-layouts: 10.2 us -> none  [spread(): jnp.where(lax.axis_index(axis) == source, value, 0).astype(value.dtype)]
  transfers between devices with their start and end apart: 7 -> 38, of which waited for: 7 -> 24; matrix products, arithmetic and copies ran while one was open for 14% -> 2% of each run, Pallas kernels for 0% -> 12%
where the time goes in v1:
time: 217 us; the launch traced here: 216 us
  waiting for transfers between devices  90.4 us (42%)
  starting transfers between devices  65.1 us (30%)
  Pallas kernels  39.2 us (18%)
  between operations  14 us (6%)
  other arithmetic  4.53 us (2%)
  local copies, waits for them, and re-layouts  2.87 us (1%)
    ppermute x35, waiting for transfers between devices, send(): return lax.ppermute(value, AXES, pairs)  85.9 us
    ppermute x35, starting transfers between devices, send(): return lax.ppermute(value, AXES, pairs)  65 us
    pallas_call x6, Pallas kernels, call(): pl.pallas_call(body, out_shape=outs, in_specs=[pl.BlockSpec(memory_space=...  38.7 us
    all_gather x1, waiting for transfers between devices, local(): lax.all_gather(sigma, 'col')  4.46 us
  transfers between devices with their start and end apart: 38, of which 24 were waited for; matrix products, arithmetic and copies ran while one was open for 2% of the time, Pallas kernels for 12%

profile of v1, /device:TPU:0, one launch (start us, length us, event | category | flops | bytes accessed | tf_op | source)
XLA Modules:
  0.0 216.1 jit_solution(1060455610747060806)
XLA Ops:
  7.2 3.2 %shard_map.67 = (f32[128,512]{1,0:T(8,128)}, f32[128,512]{1,0:T(8,128)}, f32[128,256]{1,0:T(8,128)}, f32[512,256]{1,0:T(8,128)}, f32[384,128]{1,0:T(8,128)}, /*index=5*/f32[384,128]{1,0:T(8,128)}) custom-call(s32[2,32]{1,0:T(2,128)} %refs_0_.3, f32[1024,128]{1,0:T(8,128)} %bitcast.14, f32[1024,128]{1,0:T(8,128)} %bitcast.15, f32[512,128]{1,0:T(8,128)} %bitcast.12), custom_call_target="tpu_custom_call" | custom-call | bytes 4194304 | tf_op jit(solution)/shard_map/pallas_call | solution.py:146
  13.4 5.3 %collective-permute-done.5 = f32[128,256]{1,0:T(8,128)S(1)} collective-permute-done((f32[128,256]{1,0:T(8,128)}, f32[128,256]{1,0:T(8,128)S(1)}, u32[]{:S(2)}, u32[]{:S(2)}) %collective-permute-start.5) | collective-permute-done | bytes 131104 | tf_op jit(solution)/shard_map/ppermute | solution.py:49
  19.8 2.3 %collective-permute-start.6 = (f32[128,512]{1,0:T(8,128)S(1)}, f32[128,512]{1,0:T(8,128)S(1)}, u32[]{:S(2)}, u32[]{:S(2)}) collective-permute-start(f32[128,512]{1,0:T(8,128)S(1)} %pad_maximum_fusion.1.refs_4_), channel_id=1, source_target_pairs={{0,8},{1,25},{2,10},{3,27},{4,12},{5,29},{6,14},{7,31},{8,16},{9,1... | collective-permute-start | bytes 786440 | tf_op jit(solution)/shard_map/ppermute | solution.py:49
  24.8 7.3 %collective-permute-start.2 = (f32[128,512]{1,0:T(8,128)}, f32[128,512]{1,0:T(8,128)S(1)}, u32[]{:S(2)}, u32[]{:S(2)}) collective-permute-start(f32[128,512]{1,0:T(8,128)} %get-tuple-element.30.refs_0_), channel_id=1, source_target_pairs={{0,96},{1,33},{2,98},{3,35},{4,100},{5,37},{6,102},{7,39},{8,104},... | collective-permute-start | bytes 786440 | tf_op jit(solution)/shard_map/ppermute | solution.py:49
  32.1 6.3 %collective-permute-start.7 = (f32[128,512]{1,0:T(8,128)S(1)}, f32[128,512]{1,0:T(8,128)S(1)}, u32[]{:S(2)}, u32[]{:S(2)}) collective-permute-start(f32[128,512]{1,0:T(8,128)S(1)} %pad_maximum_fusion.1.refs_4_), channel_id=1, source_target_pairs={{0,24},{1,9},{2,26},{3,11},{4,28},{5,13},{6,30},{7,15},{8,0},{9,17... | collective-permute-start | bytes 786440 | tf_op jit(solution)/shard_map/ppermute | solution.py:49
  42.5 5.0 %collective-permute-done.4.refs_3_ = f32[128,512]{1,0:T(8,128)S(1)} collective-permute-done((f32[128,512]{1,0:T(8,128)S(1)}, f32[128,512]{1,0:T(8,128)S(1)}, u32[]{:S(2)}, u32[]{:S(2)}) %collective-permute-start.4) | collective-permute-done | bytes 262176 | tf_op jit(solution)/shard_map/ppermute | solution.py:49
  54.2 2.8 %collective-permute-start.10 = (f32[512,512]{1,0:T(8,128)S(1)}, f32[512,512]{1,0:T(8,128)}, u32[]{:S(2)}, u32[]{:S(2)}) collective-permute-start(f32[512,512]{1,0:T(8,128)S(1)} %get-tuple-element.36.refs_2_.refs_1_), channel_id=1, source_target_pairs={{0,24},{1,9},{2,26},{3,11},{4,28},{5,13},{6,30},{7,15},{8,0},{9,17... | collective-permute-start | bytes 3145736 | tf_op jit(solution)/shard_map/ppermute | solution.py:49
  58.0 16.8 %collective-permute-done.9.refs_3_.refs_2_ = f32[512,512]{1,0:T(8,128)S(1)} collective-permute-done((f32[512,512]{1,0:T(8,128)S(1)}, f32[512,512]{1,0:T(8,128)S(1)}, u32[]{:S(2)}, u32[]{:S(2)}) %collective-permute-start.9) | collective-permute-done | bytes 1048608 | tf_op jit(solution)/shard_map/ppermute | solution.py:49
  74.8 3.9 %collective-permute-start.11 = (f32[512,512]{1,0:T(8,128)S(1)}, f32[512,512]{1,0:T(8,128)}, u32[]{:S(2)}, u32[]{:S(2)}) collective-permute-start(f32[512,512]{1,0:T(8,128)S(1)} %collective-permute-done.9.refs_3_.refs_2_), channel_id=1, source_target_pairs={{0,8},{1,25},{2,10},{3,27},{4,12},{5,29},{6,14},{7,31},{8,16},{9,1... | collective-permute-start | bytes 3145736 | tf_op jit(solution)/shard_map/ppermute | solution.py:49
  79.8 5.3 %shard_map.69 = (bf16[2,256,2048]{2,1,0:T(8,128)(2,1)}, bf16[2,256,2048]{2,1,0:T(8,128)(2,1)}) custom-call(f32[8,512,256]{2,1,0:T(8,128)} %bitcast.9), custom_call_target="tpu_custom_call" | custom-call | flops 1048576 | bytes 4194304 | tf_op jit(solution)/shard_map/pallas_call | solution.py:146
  85.2 7.1 %collective-permute-done.11.refs_5_.refs_4_ = f32[512,512]{1,0:T(8,128)} collective-permute-done((f32[512,512]{1,0:T(8,128)S(1)}, f32[512,512]{1,0:T(8,128)}, u32[]{:S(2)}, u32[]{:S(2)}) %collective-permute-start.11) | collective-permute-done | bytes 1048608 | tf_op jit(solution)/shard_map/ppermute | solution.py:49
  92.3 2.7 %collective-permute-done.14.refs_9_.refs_8_ = f32[512,512]{1,0:T(8,128)} collective-permute-done((f32[512,512]{1,0:T(8,128)}, f32[512,512]{1,0:T(8,128)}, u32[]{:S(2)}, u32[]{:S(2)}) %collective-permute-start.14) | collective-permute-done | bytes 1048608 | tf_op jit(solution)/shard_map/ppermute | solution.py:49
  95.0 6.7 %shard_map.70 = (f32[128,512]{1,0:T(8,128)}, f32[128,512]{1,0:T(8,128)}) custom-call(bf16[2,256,2048]{2,1,0:T(8,128)(2,1)} %get-tuple-element.40.refs_0_, bf16[2,256,2048]{2,1,0:T(8,128)(2,1)} %get-tuple-element.41.refs_1_, f32[512,512]{1,0:T(8,128)} %copy-done, f32[512,512]{1,0:T(8,128)} %copy-done.7, f32[512,512]{1,0:T(8,128)} %collective-permute-done.10.refs_4_.refs_3_, ...), custom_call_target="tpu_custom_call" | custom-call | flops 2147483648 | bytes 4194304 | tf_op jit(solution)/shard_map/pallas_call | solution.py:146
  102.0 4.0 %collective-permute-start.18 = (f32[128,512]{1,0:T(8,128)}, f32[128,512]{1,0:T(8,128)S(1)}, u32[]{:S(2)}, u32[]{:S(2)}) collective-permute-start(f32[128,512]{1,0:T(8,128)} %get-tuple-element.44.refs_4_.refs_7_), channel_id=1, source_target_pairs={{0,8},{1,25},{2,10},{3,27},{4,12},{5,29},{6,14},{7,31},{8,16},{9,1... | collective-permute-start | bytes 786440 | tf_op jit(solution)/shard_map/ppermute | solution.py:49
  106.0 3.2 %collective-permute-start.16 = (f32[128,512]{1,0:T(8,128)}, f32[128,512]{1,0:T(8,128)S(1)}, u32[]{:S(2)}, u32[]{:S(2)}) collective-permute-start(f32[128,512]{1,0:T(8,128)} %get-tuple-element.43.refs_0_.refs_6_), channel_id=1, source_target_pairs={{0,96},{1,33},{2,98},{3,35},{4,100},{5,37},{6,102},{7,39},{8,104},... | collective-permute-start | bytes 786440 | tf_op jit(solution)/shard_map/ppermute | solution.py:49
  109.2 3.1 %collective-permute-done.15.refs_1_ = f32[128,512]{1,0:T(8,128)S(1)} collective-permute-done((f32[128,512]{1,0:T(8,128)}, f32[128,512]{1,0:T(8,128)S(1)}, u32[]{:S(2)}, u32[]{:S(2)}) %collective-permute-start.15) | collective-permute-done | bytes 262176 | tf_op jit(solution)/shard_map/ppermute | solution.py:49
  115.5 2.1 collective-permute-done.19.refs_6_
  117.6 2.3 %collective-permute-done.17.refs_3_ = f32[128,512]{1,0:T(8,128)S(1)} collective-permute-done((f32[128,512]{1,0:T(8,128)S(1)}, f32[128,512]{1,0:T(8,128)S(1)}, u32[]{:S(2)}, u32[]{:S(2)}) %collective-permute-start.17) | collective-permute-done | bytes 262176 | tf_op jit(solution)/shard_map/ppermute | solution.py:49
  126.3 2.4 %collective-permute-start.24 = (f32[512,512]{1,0:T(8,128)S(1)}, f32[512,512]{1,0:T(8,128)}, u32[]{:S(2)}, u32[]{:S(2)}) collective-permute-start(f32[512,512]{1,0:T(8,128)S(1)} %get-tuple-element.49.refs_3_), channel_id=1, source_target_pairs={{0,96},{1,33},{2,98},{3,35},{4,100},{5,37},{6,102},{7,39},{8,104},... | collective-permute-start | bytes 3145736 | tf_op jit(solution)/shard_map/ppermute | solution.py:49
  128.7 7.8 %shard_map.72 = (f32[256,512]{1,0:T(8,128)}, f32[1024,128]{1,0:T(8,128)}) custom-call(f32[8,768,128]{2,1,0:T(8,128)} %bitcast.11, f32[512,512]{1,0:T(8,128)} %copy-done, f32[512,512]{1,0:T(8,128)} %copy-done.7, f32[512,512]{1,0:T(8,128)} %collective-permute-done.10.refs_4_.refs_3_, f32[512,512]{1,0:T(8,128)} %collective-permute-done.11.refs_5_.refs_4_, ...), custom_call_target="tpu_custom_call" | custom-call | flops 2147483648 | bytes 4194304 | tf_op jit(solution)/shard_map/pallas_call | solution.py:146
  136.6 10.8 %collective-permute-done.21.refs_1_ = f32[512,512]{1,0:T(8,128)} collective-permute-done((f32[512,512]{1,0:T(8,128)S(1)}, f32[512,512]{1,0:T(8,128)}, u32[]{:S(2)}, u32[]{:S(2)}) %collective-permute-start.21) | collective-permute-done | bytes 1048608 | tf_op jit(solution)/shard_map/ppermute | solution.py:49
  148.3 5.7 %shard_map.73 = (bf16[3072,512]{1,0:T(8,128)(2,1)}, bf16[3072,512]{1,0:T(8,128)(2,1)}) custom-call(f32[512,512]{1,0:T(8,128)} %copy-done.5, f32[512,512]{1,0:T(8,128)} %collective-permute-done.21.refs_1_, f32[512,512]{1,0:T(8,128)} %collective-permute-done.22.refs_2_, f32[512,512]{1,0:T(8,128)} %copy-done.6, f32[512,512]{1,0:T(8,128)} %collective-permute-done.23.refs_4_, ...), custom_call_target="tpu_custom_call" | custom-call | flops 68719476736 | bytes 4194304 | tf_op jit(solution)/shard_map/pallas_call | solution.py:146
  153.9 9.7 %collective-permute-done.25.refs_4_ = f32[512,512]{1,0:T(8,128)S(1)} collective-permute-done((f32[512,512]{1,0:T(8,128)}, f32[512,512]{1,0:T(8,128)S(1)}, u32[]{:S(2)}, u32[]{:S(2)}) %collective-permute-start.25) | collective-permute-done | bytes 1048608 | tf_op jit(solution)/shard_map/ppermute | solution.py:49
  164.6 4.5 %all-gather.11.cloned.1.call-done = f32[2048,512]{1,0:T(8,128)} async-done(((f32[256,512]{1,0:T(8,128)}), f32[2048,512]{1,0:T(8,128)}) %all-gather.11.cloned.1.call-update) | async-done | bytes 4194320 | tf_op jit(solution)/shard_map/all_gather | solution.py:330
  169.0 10.1 %shard_map.74 = (f32[1024,128]{1,0:T(8,128)}, f32[256,128]{1,0:T(8,128)}, f32[256,128]{1,0:T(8,128)}) custom-call(s32[2,32]{1,0:T(2,128)} %refs_0_.3, f32[8,256,512]{2,1,0:T(8,128)} %bitcast.10, bf16[3072,512]{1,0:T(8,128)(2,1)} %get-tuple-element.50.refs_2_, bf16[3072,512]{1,0:T(8,128)(2,1)} %get-tuple-element.51.refs_3_, f32[512,512]{1,0:T(8,128)} %copy-done.8, ...), custom_call_target="tpu_custom_call" | custom-call | flops 1073741824 | bytes 4194304 | tf_op jit(solution)/shard_map/pallas_call | solution.py:146
  182.2 2.2 collective-permute-done.31
  185.3 3.0 %collective-permute-start.32 = (f32[256,128]{1,0:T(8,128)S(1)}, f32[256,128]{1,0:T(8,128)S(1)}, u32[]{:S(2)}, u32[]{:S(2)}) collective-permute-start(f32[256,128]{1,0:T(8,128)S(1)} %add.28), channel_id=1, source_target_pairs={{0,24},{1,9},{2,26},{3,11},{4,28},{5,13},{6,30},{7,15},{8,16},{9,1... | collective-permute-start | bytes 393224 | tf_op jit(solution)/shard_map/ppermute | solution.py:49
  189.2 2.8 %collective-permute-start.28 = (f32[256,128]{1,0:T(8,128)S(1)}, f32[256,128]{1,0:T(8,128)S(1)}, u32[]{:S(2)}, u32[]{:S(2)}) collective-permute-start(f32[256,128]{1,0:T(8,128)S(1)} %add.24), channel_id=1, source_target_pairs={{0,96},{1,33},{2,98},{3,35},{4,100},{5,37},{6,102},{7,39},{8,104},... | collective-permute-start | bytes 393224 | tf_op jit(solution)/shard_map/ppermute | solution.py:49
  193.1 3.1 %collective-permute-done.28 = f32[256,128]{1,0:T(8,128)S(1)} collective-permute-done((f32[256,128]{1,0:T(8,128)S(1)}, f32[256,128]{1,0:T(8,128)S(1)}, u32[]{:S(2)}, u32[]{:S(2)}) %collective-permute-start.28) | collective-permute-done | bytes 131104 | tf_op jit(solution)/shard_map/ppermute | solution.py:49
  197.1 2.6 %collective-permute-start.34 = (f32[256,128]{1,0:T(8,128)S(1)}, f32[256,128]{1,0:T(8,128)S(1)}, u32[]{:S(2)}, u32[]{:S(2)}) collective-permute-start(f32[256,128]{1,0:T(8,128)S(1)} %add.30), channel_id=1, source_target_pairs={{0,96},{1,33},{2,98},{3,35},{4,100},{5,37},{6,102},{7,39},{8,104},... | collective-permute-start | bytes 393224 | tf_op jit(solution)/shard_map/ppermute | solution.py:49
  199.7 2.8 %collective-permute-done.29 = f32[256,128]{1,0:T(8,128)S(1)} collective-permute-done((f32[256,128]{1,0:T(8,128)S(1)}, f32[256,128]{1,0:T(8,128)S(1)}, u32[]{:S(2)}, u32[]{:S(2)}) %collective-permute-start.29) | collective-permute-done | bytes 131104 | tf_op jit(solution)/shard_map/ppermute | solution.py:49
  203.4 5.5 %collective-permute-done.30 = f32[256,128]{1,0:T(8,128)S(1)} collective-permute-done((f32[256,128]{1,0:T(8,128)S(1)}, f32[256,128]{1,0:T(8,128)S(1)}, u32[]{:S(2)}, u32[]{:S(2)}) %collective-permute-start.30) | collective-permute-done | bytes 131104 | tf_op jit(solution)/shard_map/ppermute | solution.py:49
  (85 shorter events, 39.8 us)
Async XLA Ops:
  7.2 72.7 %all-gather.9.cloned.1.call-start = ((), (), s32[]{:S(2)}) async-start(), calls=%async_computation.1 | async-start | bytes 4718592 | tf_op jit(solution)/shard_map/all_gather | solution.py:304
  10.4 118.3 %all-gather.7.cloned.1.call-start = ((), (), s32[]{:S(2)}) async-start(), calls=%async_computation | async-start | bytes 3538944 | tf_op jit(solution)/shard_map/all_gather | solution.py:303
  10.5 8.3 %collective-permute-start.5 = (f32[128,256]{1,0:T(8,128)}, f32[128,256]{1,0:T(8,128)S(1)}, u32[]{:S(2)}, u32[]{:S(2)}) collective-permute-start(f32[128,256]{1,0:T(8,128)} %get-tuple-element.34), channel_id=1, source_target_pairs={{64,32},{65,33},{66,34},{67,35},{68,36},{69,37},{70,38},{71,39},{7... | collective-permute-start | bytes 393224 | tf_op jit(solution)/shard_map/ppermute | solution.py:49
  11.8 26.6 %collective-permute-start.1 = (f32[128,512]{1,0:T(8,128)}, f32[128,512]{1,0:T(8,128)S(1)}, u32[]{:S(2)}, u32[]{:S(2)}) collective-permute-start(f32[128,512]{1,0:T(8,128)} %get-tuple-element.30.refs_0_), channel_id=1, source_target_pairs={{0,32},{1,97},{2,34},{3,99},{4,36},{5,101},{6,38},{7,103},{8,40},{... | collective-permute-start | bytes 786440 | tf_op jit(solution)/shard_map/ppermute | solution.py:49
  19.8 20.5 %collective-permute-start.6 = (f32[128,512]{1,0:T(8,128)S(1)}, f32[128,512]{1,0:T(8,128)S(1)}, u32[]{:S(2)}, u32[]{:S(2)}) collective-permute-start(f32[128,512]{1,0:T(8,128)S(1)} %pad_maximum_fusion.1.refs_4_), channel_id=1, source_target_pairs={{0,8},{1,25},{2,10},{3,27},{4,12},{5,29},{6,14},{7,31},{8,16},{9,1... | collective-permute-start | bytes 786440 | tf_op jit(solution)/shard_map/ppermute | solution.py:49
  22.1 10.0 %collective-permute-start.3 = (f32[384,128]{1,0:T(8,128)}, f32[384,128]{1,0:T(8,128)S(1)}, u32[]{:S(2)}, u32[]{:S(2)}) collective-permute-start(f32[384,128]{1,0:T(8,128)} %get-tuple-element.31), channel_id=1, source_target_pairs={{0,64},{1,72},{2,80},{3,88},{4,96},{5,104},{6,112},{7,120},{8,0},{... | collective-permute-start | bytes 589832 | tf_op jit(solution)/shard_map/ppermute | solution.py:49
  23.2 15.2 %collective-permute-start = (f32[384,128]{1,0:T(8,128)}, f32[384,128]{1,0:T(8,128)S(1)}, u32[]{:S(2)}, u32[]{:S(2)}) collective-permute-start(f32[384,128]{1,0:T(8,128)} %get-tuple-element.29), channel_id=1, source_target_pairs={{0,0},{1,8},{2,16},{3,24},{4,32},{5,40},{6,48},{7,56},{8,64},{9,72... | collective-permute-start | bytes 589832 | tf_op jit(solution)/shard_map/ppermute | solution.py:49
  24.8 16.3 %collective-permute-start.2 = (f32[128,512]{1,0:T(8,128)}, f32[128,512]{1,0:T(8,128)S(1)}, u32[]{:S(2)}, u32[]{:S(2)}) collective-permute-start(f32[128,512]{1,0:T(8,128)} %get-tuple-element.30.refs_0_), channel_id=1, source_target_pairs={{0,96},{1,33},{2,98},{3,35},{4,100},{5,37},{6,102},{7,39},{8,104},... | collective-permute-start | bytes 786440 | tf_op jit(solution)/shard_map/ppermute | solution.py:49
  32.1 10.4 %collective-permute-start.7 = (f32[128,512]{1,0:T(8,128)S(1)}, f32[128,512]{1,0:T(8,128)S(1)}, u32[]{:S(2)}, u32[]{:S(2)}) collective-permute-start(f32[128,512]{1,0:T(8,128)S(1)} %pad_maximum_fusion.1.refs_4_), channel_id=1, source_target_pairs={{0,24},{1,9},{2,26},{3,11},{4,28},{5,13},{6,30},{7,15},{8,0},{9,17... | collective-permute-start | bytes 786440 | tf_op jit(solution)/shard_map/ppermute | solution.py:49
  38.4 9.1 %collective-permute-start.4 = (f32[128,512]{1,0:T(8,128)S(1)}, f32[128,512]{1,0:T(8,128)S(1)}, u32[]{:S(2)}, u32[]{:S(2)}) collective-permute-start(f32[128,512]{1,0:T(8,128)S(1)} %collective-permute-done.1.refs_1_), channel_id=1, source_target_pairs={{0,32},{1,97},{2,34},{3,99},{4,36},{5,101},{6,38},{7,103},{8,40},{... | collective-permute-start | bytes 786440 | tf_op jit(solution)/shard_map/ppermute | solution.py:49
  40.3 8.8 %collective-permute-start.8 = (f32[128,512]{1,0:T(8,128)S(1)}, f32[128,512]{1,0:T(8,128)S(1)}, u32[]{:S(2)}, u32[]{:S(2)}) collective-permute-start(f32[128,512]{1,0:T(8,128)S(1)} %collective-permute-done.6.refs_5_), channel_id=1, source_target_pairs={{0,8},{1,25},{2,10},{3,27},{4,12},{5,29},{6,14},{7,31},{8,16},{9,1... | collective-permute-start | bytes 786440 | tf_op jit(solution)/shard_map/ppermute | solution.py:49
  51.2 117.8 %all-gather.11.cloned.1.call-start = ((), (), s32[]{:S(2)}) async-start(), calls=%async_computation.2 | async-start | bytes 4718592 | tf_op jit(solution)/shard_map/all_gather | solution.py:330
  51.3 23.5 %collective-permute-start.9 = (f32[512,512]{1,0:T(8,128)S(1)}, f32[512,512]{1,0:T(8,128)S(1)}, u32[]{:S(2)}, u32[]{:S(2)}) collective-permute-start(f32[512,512]{1,0:T(8,128)S(1)} %get-tuple-element.36.refs_2_.refs_1_), channel_id=1, source_target_pairs={{0,8},{1,25},{2,10},{3,27},{4,12},{5,29},{6,14},{7,31},{8,16},{9,1... | collective-permute-start | bytes 3145736 | tf_op jit(solution)/shard_map/ppermute | solution.py:49
  53.0 25.7 %collective-permute-start.12 = (f32[512,512]{1,0:T(8,128)S(1)}, f32[512,512]{1,0:T(8,128)}, u32[]{:S(2)}, u32[]{:S(2)}) collective-permute-start(f32[512,512]{1,0:T(8,128)S(1)} %get-tuple-element.42.refs_6_.refs_5_), channel_id=1, source_target_pairs={{0,32},{1,97},{2,34},{3,99},{4,36},{5,101},{6,38},{7,103},{8,40},{... | collective-permute-start | bytes 3145736 | tf_op jit(solution)/shard_map/ppermute | solution.py:49
  54.2 31.0 %collective-permute-start.10 = (f32[512,512]{1,0:T(8,128)S(1)}, f32[512,512]{1,0:T(8,128)}, u32[]{:S(2)}, u32[]{:S(2)}) collective-permute-start(f32[512,512]{1,0:T(8,128)S(1)} %get-tuple-element.36.refs_2_.refs_1_), channel_id=1, source_target_pairs={{0,24},{1,9},{2,26},{3,11},{4,28},{5,13},{6,30},{7,15},{8,0},{9,17... | collective-permute-start | bytes 3145736 | tf_op jit(solution)/shard_map/ppermute | solution.py:49
  57.0 28.2 %collective-permute-start.13 = (f32[512,512]{1,0:T(8,128)S(1)}, f32[512,512]{1,0:T(8,128)}, u32[]{:S(2)}, u32[]{:S(2)}) collective-permute-start(f32[512,512]{1,0:T(8,128)S(1)} %get-tuple-element.42.refs_6_.refs_5_), channel_id=1, source_target_pairs={{0,96},{1,33},{2,98},{3,35},{4,100},{5,37},{6,102},{7,39},{8,104},... | collective-permute-start | bytes 3145736 | tf_op jit(solution)/shard_map/ppermute | solution.py:49
  74.8 17.5 %collective-permute-start.11 = (f32[512,512]{1,0:T(8,128)S(1)}, f32[512,512]{1,0:T(8,128)}, u32[]{:S(2)}, u32[]{:S(2)}) collective-permute-start(f32[512,512]{1,0:T(8,128)S(1)} %collective-permute-done.9.refs_3_.refs_2_), channel_id=1, source_target_pairs={{0,8},{1,25},{2,10},{3,27},{4,12},{5,29},{6,14},{7,31},{8,16},{9,1... | collective-permute-start | bytes 3145736 | tf_op jit(solution)/shard_map/ppermute | solution.py:49
  78.7 16.3 %collective-permute-start.14 = (f32[512,512]{1,0:T(8,128)}, f32[512,512]{1,0:T(8,128)}, u32[]{:S(2)}, u32[]{:S(2)}) collective-permute-start(f32[512,512]{1,0:T(8,128)} %collective-permute-done.12.refs_7_.refs_6_), channel_id=1, source_target_pairs={{0,32},{1,97},{2,34},{3,99},{4,36},{5,101},{6,38},{7,103},{8,40},{... | collective-permute-start | bytes 3145736 | tf_op jit(solution)/shard_map/ppermute | solution.py:49
  101.8 10.6 %collective-permute-start.15 = (f32[128,512]{1,0:T(8,128)}, f32[128,512]{1,0:T(8,128)S(1)}, u32[]{:S(2)}, u32[]{:S(2)}) collective-permute-start(f32[128,512]{1,0:T(8,128)} %get-tuple-element.43.refs_0_.refs_6_), channel_id=1, source_target_pairs={{0,32},{1,97},{2,34},{3,99},{4,36},{5,101},{6,38},{7,103},{8,40},{... | collective-permute-start | bytes 786440 | tf_op jit(solution)/shard_map/ppermute | solution.py:49
  102.0 10.4 %collective-permute-start.18 = (f32[128,512]{1,0:T(8,128)}, f32[128,512]{1,0:T(8,128)S(1)}, u32[]{:S(2)}, u32[]{:S(2)}) collective-permute-start(f32[128,512]{1,0:T(8,128)} %get-tuple-element.44.refs_4_.refs_7_), channel_id=1, source_target_pairs={{0,8},{1,25},{2,10},{3,27},{4,12},{5,29},{6,14},{7,31},{8,16},{9,1... | collective-permute-start | bytes 786440 | tf_op jit(solution)/shard_map/ppermute | solution.py:49
  106.0 9.4 %collective-permute-start.16 = (f32[128,512]{1,0:T(8,128)}, f32[128,512]{1,0:T(8,128)S(1)}, u32[]{:S(2)}, u32[]{:S(2)}) collective-permute-start(f32[128,512]{1,0:T(8,128)} %get-tuple-element.43.refs_0_.refs_6_), channel_id=1, source_target_pairs={{0,96},{1,33},{2,98},{3,35},{4,100},{5,37},{6,102},{7,39},{8,104},... | collective-permute-start | bytes 786440 | tf_op jit(solution)/shard_map/ppermute | solution.py:49
  109.2 8.4 %collective-permute-start.19 = (f32[128,512]{1,0:T(8,128)}, f32[128,512]{1,0:T(8,128)S(1)}, u32[]{:S(2)}, u32[]{:S(2)}) collective-permute-start(f32[128,512]{1,0:T(8,128)} %get-tuple-element.44.refs_4_.refs_7_), channel_id=1, source_target_pairs={{0,24},{1,9},{2,26},{3,11},{4,28},{5,13},{6,30},{7,15},{8,0},{9,17... | collective-permute-start | bytes 786440 | tf_op jit(solution)/shard_map/ppermute | solution.py:49
  112.3 7.6 %collective-permute-start.17 = (f32[128,512]{1,0:T(8,128)S(1)}, f32[128,512]{1,0:T(8,128)S(1)}, u32[]{:S(2)}, u32[]{:S(2)}) collective-permute-start(f32[128,512]{1,0:T(8,128)S(1)} %collective-permute-done.15.refs_1_), channel_id=1, source_target_pairs={{0,32},{1,97},{2,34},{3,99},{4,36},{5,101},{6,38},{7,103},{8,40},{... | collective-permute-start | bytes 786440 | tf_op jit(solution)/shard_map/ppermute | solution.py:49
  112.4 7.6 %collective-permute-start.20 = (f32[128,512]{1,0:T(8,128)S(1)}, f32[128,512]{1,0:T(8,128)S(1)}, u32[]{:S(2)}, u32[]{:S(2)}) collective-permute-start(f32[128,512]{1,0:T(8,128)S(1)} %collective-permute-done.18.refs_5_), channel_id=1, source_target_pairs={{0,8},{1,25},{2,10},{3,27},{4,12},{5,29},{6,14},{7,31},{8,16},{9,1... | collective-permute-start | bytes 786440 | tf_op jit(solution)/shard_map/ppermute | solution.py:49
  122.2 25.2 %collective-permute-start.21 = (f32[512,512]{1,0:T(8,128)S(1)}, f32[512,512]{1,0:T(8,128)}, u32[]{:S(2)}, u32[]{:S(2)}) collective-permute-start(f32[512,512]{1,0:T(8,128)S(1)} %get-tuple-element.45.refs_0_), channel_id=1, source_target_pairs={{0,8},{1,25},{2,10},{3,27},{4,12},{5,29},{6,14},{7,31},{8,16},{9,1... | collective-permute-start | bytes 3145736 | tf_op jit(solution)/shard_map/ppermute | solution.py:49
  123.9 24.4 %collective-permute-start.22 = (f32[512,512]{1,0:T(8,128)S(1)}, f32[512,512]{1,0:T(8,128)}, u32[]{:S(2)}, u32[]{:S(2)}) collective-permute-start(f32[512,512]{1,0:T(8,128)S(1)} %get-tuple-element.45.refs_0_), channel_id=1, source_target_pairs={{0,24},{1,9},{2,26},{3,11},{4,28},{5,13},{6,30},{7,15},{8,0},{9,17... | collective-permute-start | bytes 3145736 | tf_op jit(solution)/shard_map/ppermute | solution.py:49
  125.5 22.8 %collective-permute-start.23 = (f32[512,512]{1,0:T(8,128)S(1)}, f32[512,512]{1,0:T(8,128)}, u32[]{:S(2)}, u32[]{:S(2)}) collective-permute-start(f32[512,512]{1,0:T(8,128)S(1)} %get-tuple-element.49.refs_3_), channel_id=1, source_target_pairs={{0,32},{1,97},{2,34},{3,99},{4,36},{5,101},{6,38},{7,103},{8,40},{... | collective-permute-start | bytes 3145736 | tf_op jit(solution)/shard_map/ppermute | solution.py:49
  126.3 22.0 %collective-permute-start.24 = (f32[512,512]{1,0:T(8,128)S(1)}, f32[512,512]{1,0:T(8,128)}, u32[]{:S(2)}, u32[]{:S(2)}) collective-permute-start(f32[512,512]{1,0:T(8,128)S(1)} %get-tuple-element.49.refs_3_), channel_id=1, source_target_pairs={{0,96},{1,33},{2,98},{3,35},{4,100},{5,37},{6,102},{7,39},{8,104},... | collective-permute-start | bytes 3145736 | tf_op jit(solution)/shard_map/ppermute | solution.py:49
  147.4 16.2 %collective-permute-start.25 = (f32[512,512]{1,0:T(8,128)}, f32[512,512]{1,0:T(8,128)S(1)}, u32[]{:S(2)}, u32[]{:S(2)}) collective-permute-start(f32[512,512]{1,0:T(8,128)} %collective-permute-done.21.refs_1_), channel_id=1, source_target_pairs={{0,8},{1,25},{2,10},{3,27},{4,12},{5,29},{6,14},{7,31},{8,16},{9,1... | collective-permute-start | bytes 3145736 | tf_op jit(solution)/shard_map/ppermute | solution.py:49
  148.3 16.3 %collective-permute-start.26 = (f32[512,512]{1,0:T(8,128)}, f32[512,512]{1,0:T(8,128)}, u32[]{:S(2)}, u32[]{:S(2)}) collective-permute-start(f32[512,512]{1,0:T(8,128)} %collective-permute-done.23.refs_4_), channel_id=1, source_target_pairs={{0,32},{1,97},{2,34},{3,99},{4,36},{5,101},{6,38},{7,103},{8,40},{... | collective-permute-start | bytes 3145736 | tf_op jit(solution)/shard_map/ppermute | solution.py:49
  180.7 7.6 %collective-permute-start.27 = (f32[256,128]{1,0:T(8,128)}, f32[256,128]{1,0:T(8,128)S(1)}, u32[]{:S(2)}, u32[]{:S(2)}) collective-permute-start(f32[256,128]{1,0:T(8,128)} %get-tuple-element.53), channel_id=1, source_target_pairs={{0,32},{1,97},{2,34},{3,99},{4,36},{5,101},{6,38},{7,103},{8,40},{... | collective-permute-start | bytes 393224 | tf_op jit(solution)/shard_map/ppermute | solution.py:49
  189.2 7.0 %collective-permute-start.28 = (f32[256,128]{1,0:T(8,128)S(1)}, f32[256,128]{1,0:T(8,128)S(1)}, u32[]{:S(2)}, u32[]{:S(2)}) collective-permute-start(f32[256,128]{1,0:T(8,128)S(1)} %add.24), channel_id=1, source_target_pairs={{0,96},{1,33},{2,98},{3,35},{4,100},{5,37},{6,102},{7,39},{8,104},... | collective-permute-start | bytes 393224 | tf_op jit(solution)/shard_map/ppermute | solution.py:49
  (15 other events, 182.5 us)
Sparse Core Ops, SparseCore 0:
  10.6 41.9 all-gather.8
  54.8 27.7 all-gather.6
  136.7 32.3 all-gather.10
